TPU v7x, 32 devices: a whole 2x2x4 slice. The times are simulated.
32 devices in a mesh: blk: 8 (over z, y), group: 4 (over x, core).
Axes of the slice: x: 2, y: 2, z: 4, core: 2. Of those that a mesh axis runs over, the one named last changes fastest.
Arguments:
- image_embeds: bfloat16 [4, 768, 1152], P('group', 'blk')
- text_embeds: bfloat16 [4, 768, 1152], P('group', 'blk'), may hold values from -0.1875 to 0.1875
- positives: int32 [4, 768], P('group', 'blk'), may hold values from 0 to 767, each once within a row
- partner: int32 [4], replicated, may hold values from 0 to 3, each once
- log_temp: float32 [1], replicated, may hold values from 1.6 to 2.4
- bias: float32 [1], replicated, may hold values from -4 to -2
Outputs:
- image_grads: float32 [4, 768, 1152], P('group', 'blk')
- text_grads: float32 [4, 768, 1152], P('group', 'blk')
- loss: float32 [1], replicated
Inputs may be any that keep to these rules, and one draw needn't show every extreme that they name: Each group's positives name every text row of its partner group exactly once. `partner`: every group is named exactly once.
All inputs are finite; a program needn't handle non-finite values.
Results may differ from a plain program's by a relative error of at most 0.0015.
Values may be sent and summed in bfloat16 or wider, within the bound.
No kernel may reach another device: no remote copies, remote signals or barrier semaphores. Data moves between devices by JAX's collectives and lax.ppermute only.
A program may use at most 64 MiB of HBM per device.

v0:
```python
import jax
import jax.numpy as jnp
from jax import lax
from jax.sharding import PartitionSpec as P

RING = {0: 2, 2: 3, 3: 1, 1: 0}
TAIL = 16
DIGIT = 128


def pair_slopes(rows, others, hits, temper, offset):
    logits = temper * jnp.dot(rows, others.T, preferred_element_type=jnp.float32) + offset
    hit_values = hits.astype(jnp.float32)
    slopes = (jax.nn.sigmoid(logits) - hit_values).astype(jnp.bfloat16)
    return logits, hit_values, slopes


def exchange(array, axis, size, mate):
    return lax.ppermute(array, axis, [(place, mate(place)) for place in range(size)])


def swap(array, axis, size, bit):
    return exchange(array, axis, size, lambda place: place ^ bit)


def after(array, *earlier):
    return lax.optimization_barrier((array, *earlier))[0]


def pick(own, across, wanted, here, mate_wanted, groups):
    for_mate = jnp.where((mate_wanted ^ here) >> 1 == 0, own, across)
    from_mate = swap(for_mate, "group", groups, 1)
    held = jnp.where((wanted ^ here) >> 1 == 0, own, across)
    return jnp.where((wanted ^ here) & 1 == 0, held, from_mate)


def ring(array, blocks):
    return exchange(array, "blk", blocks, lambda place: 2 * RING[place // 2] + place % 2)


def ring_sources(place, blocks):
    back = {target: source for source, target in RING.items()}
    sources = [place]
    for _ in range(blocks // 2 - 1):
        here = sources[-1] // 2
        before = sum(jnp.where(here == target, source, 0) for target, source in back.items())
        sources.append(2 * before + place % 2)
    return sources


def with_labels(images, labels):
    digits = jnp.stack([labels // DIGIT, labels % DIGIT]).astype(images.dtype)
    return jnp.concatenate([images, jnp.pad(digits, ((0, TAIL - 2), (0, images.shape[1] - labels.shape[0])))])


def labels_of(block, rows):
    digits = block[rows : rows + 2, :rows].astype(jnp.int32)
    return digits[0] * DIGIT + digits[1]


def all_sum(total, axis, size, marks):
    for step in range(size.bit_length() - 1):
        if marks:
            total = after(total, marks.pop(0))
        total = total + swap(total, axis, size, 1 << step)
    return total


def shards(image_embeds, text_embeds, positives, partner, log_temp, bias):
    temper = jnp.exp(log_temp[0])
    offset = bias[0]
    texts = text_embeds[0]
    labels = positives[0]
    rows = texts.shape[0]
    blocks = lax.axis_size("blk")
    groups = lax.axis_size("group")
    blk_place = lax.axis_index("blk")
    group_place = lax.axis_index("group")
    images = with_labels(image_embeds[0], labels)

    def partner_of(group):
        return jnp.sum(jnp.where(jnp.arange(groups) == group, partner, 0))

    def scorer_of(group):
        return jnp.sum(jnp.where(partner == group, jnp.arange(groups), 0))

    def index_of(places):
        return (jnp.stack(places)[:, None] * rows + jnp.arange(rows)[None, :]).reshape(-1)

    def matches(some_labels, index):
        return some_labels[:, None] == index[None, :]

    def grads(slopes, others):
        return temper * jnp.dot(slopes, others, preferred_element_type=jnp.float32)

    scorer = scorer_of(group_place)
    texts_across = swap(texts, "group", groups, 2)
    images_across = swap(after(images, texts_across), "group", groups, 2)
    partner_text = pick(texts, texts_across, partner_of(group_place), group_place, partner_of(group_place ^ 1), groups)
    images_across = after(images_across, partner_text)
    scorer_image = pick(images, images_across, scorer, group_place, scorer_of(group_place ^ 1), groups)
    own_images = images[:rows]

    if blocks == 8:
        sources = ring_sources(blk_place, blocks)
        text_blocks = [partner_text]
        image_blocks = [scorer_image]
        relayed = [swap(scorer_image, "blk", blocks, 1)]
        mate_images = swap(images, "blk", blocks, 1)
        for _ in range(blocks // 2 - 1):
            text_blocks.append(ring(text_blocks[-1], blocks))
            image_blocks.append(ring(image_blocks[-1], blocks))
            relayed.append(swap(image_blocks[-1], "blk", blocks, 1))

        column_texts = jnp.concatenate(text_blocks)
        two_images = jnp.concatenate([own_images, mate_images[:rows]])
        two_labels = jnp.concatenate([labels, labels_of(mate_images, rows)])
        hits = matches(two_labels, index_of(sources))
        logits, hit_values, slopes = pair_slopes(two_images, column_texts, hits, temper, offset)
        total = jnp.sum(jax.nn.softplus(logits) - hit_values * logits)
        mate_part = swap(grads(slopes[rows:], column_texts), "blk", blocks, 1)
        image_grads = grads(slopes[:rows], column_texts) + mate_part

        all_blocks = image_blocks + relayed
        all_images = jnp.concatenate([block[:rows] for block in all_blocks])
        back_labels = jnp.concatenate([labels_of(block, rows) for block in all_blocks])
        marks = [column_texts, image_blocks[2], relayed[2], image_blocks[3], image_blocks[3]]
    else:
        all_texts = lax.all_gather(partner_text, "blk", axis=0, tiled=True)
        every_image = lax.all_gather(scorer_image, "blk", axis=0)
        hits = matches(labels, jnp.arange(blocks * rows))
        logits, hit_values, slopes = pair_slopes(own_images, all_texts, hits, temper, offset)
        total = jnp.sum(jax.nn.softplus(logits) - hit_values * logits)
        image_grads = grads(slopes, all_texts)
        all_images = every_image[:, :rows].reshape(blocks * rows, -1)
        back_labels = jax.vmap(lambda block: labels_of(block, rows))(every_image).reshape(-1)
        marks = []

    back_hits = index_of([blk_place])[:, None] == back_labels[None, :]
    back_slopes = pair_slopes(texts, all_images, back_hits, temper, offset)[2]
    text_grads = grads(back_slopes, all_images)

    total = jnp.full((8, 128), total)
    total = all_sum(total, "group", groups, marks)
    total = all_sum(total, "blk", blocks, marks)
    loss = total[0, :1] / (groups * rows * blocks * blocks)
    return (image_grads[None], text_grads[None], loss)


def solution(mesh):
    in_specs = (P("group", "blk", None), P("group", "blk", None), P("group", "blk"), P(), P(), P())
    out_specs = (P("group", "blk", None), P("group", "blk", None), P())
    return jax.shard_map(shards, mesh=mesh, in_specs=in_specs, out_specs=out_specs, check_vma=False)
```

profile of v0, /device:TPU:0, one launch (start us, length us, event | category | flops | bytes accessed | tf_op | source)
XLA Modules:
  0.0 81.7 jit_solution(2889573204675262385)
XLA Ops:
  0.6 3.0 %collective-permute-start.1 = (bf16[96,1152]{1,0:T(8,128)(2,1)}, bf16[96,1152]{1,0:T(8,128)(2,1)S(1)}, u32[]{:S(2)}, u32[]{:S(2)}) collective-permute-start(bf16[96,1152]{1,0:T(8,128)(2,1)} %bitcast.56), channel_id=1, source_target_pairs={{0,2},{1,3},{2,0},{3,1},{4,6},{5,7},{6,4},{7,5},{8,10},{9,11},{10,... | collective-permute-start | bytes 663560 | tf_op jit(solution)/shard_map/ppermute | solution.py:19
  3.6 0.7 fusion.39
  4.3 1.0 %pad_maximum_fusion.1 = bf16[112,1152]{1,0:T(8,128)(2,1)S(1)} fusion(bf16[16,1152]{1,0:T(8,128)(2,1)S(1)} %fusion.33, bf16[96,1152]{1,0:T(8,128)(2,1)} %bitcast.52), kind=kLoop, calls=%fused_computation.30 | loop fusion | flops 516096 | bytes 516096 | tf_op jit(solution)/shard_map/concatenate | solution.py:53
  5.3 1.6 %collective-permute-start = (bf16[112,1152]{1,0:T(8,128)(2,1)S(1)}, bf16[112,1152]{1,0:T(8,128)(2,1)S(1)}, u32[]{:S(2)}, u32[]{:S(2)}) collective-permute-start(bf16[112,1152]{1,0:T(8,128)(2,1)S(1)} %pad_maximum_fusion.1), channel_id=1, source_target_pairs={{0,4},{4,0},{8,12},{12,8},{16,20},{20,16},{24,28},{28,24},{1,5},{5... | collective-permute-start | bytes 774152 | tf_op jit(solution)/shard_map/ppermute | solution.py:19
  6.9 0.1 add_multiply_fusion
  7.0 0.1 iota_add_fusion
  7.0 1.4 %fusion.37 = (s32[]{:T(128)}, s32[]{:T(128)}, s32[]{:T(128)}, s32[]{:T(128)}) fusion(s32[4]{0:T(128)} %param.9, s32[]{:T(128)S(6)} %axis_index.22, s32[]{:T(128)S(6)} %xor.19), kind=kLoop, calls=%fused_computation.72 | loop fusion | flops 44 | bytes 40 | tf_op jit(solution)/shard_map/reduce_sum | solution.py:85
  11.1 0.1 add.198
  12.5 1.0 %broadcast_select_fusion.1 = bf16[96,1152]{1,0:T(8,128)(2,1)S(1)} fusion(bf16[96,1152]{1,0:T(8,128)(2,1)S(1)} %collective-permute-done.1, pred[]{:T(512)S(6)} %eq.106, bf16[1,96,1152]{2,1,0:T(8,128)(2,1)} %param.7), kind=kLoop, calls=%fused_computation.42 | loop fusion | flops 110592 | bytes 663553 | tf_op jit(solution)/shard_map/jit(_where)/select_n | solution.py:31
  13.5 0.1 collective-permute-start.2
  13.5 0.6 collective-permute-start.7
  14.1 0.9 %collective-permute-done.2 = bf16[96,1152]{1,0:T(8,128)(2,1)S(1)} collective-permute-done((bf16[96,1152]{1,0:T(8,128)(2,1)S(1)}, bf16[96,1152]{1,0:T(8,128)(2,1)S(1)}, u32[]{:S(2)}, u32[]{:S(2)}) %collective-permute-start.2) | collective-permute-done | bytes 221216 | tf_op jit(solution)/shard_map/ppermute | solution.py:19
  15.0 1.0 %select_select_fusion.1 = bf16[96,1152]{1,0:T(8,128)(2,1)S(1)} fusion(bf16[96,1152]{1,0:T(8,128)(2,1)S(1)} %collective-permute-done.2, bf16[96,1152]{1,0:T(8,128)(2,1)S(1)} %collective-permute-done.1, pred[]{:T(512)S(6)} %eq.103, pred[]{:T(512)S(6)} %eq.102, bf16[1,96,1152]{2,1,0:T(8,128)(2,1)} %param.7), kind=kLoop, calls=%fused_computation.41 | loop fusion | flops 221184 | bytes 884738 | tf_op jit(solution)/shard_map/jit(_where)/select_n | solution.py:34
  16.0 2.6 %collective-permute-start.3 = (bf16[96,1152]{1,0:T(8,128)(2,1)S(1)}, bf16[96,1152]{1,0:T(8,128)(2,1)S(1)}, u32[]{:S(2)}, u32[]{:S(2)}) collective-permute-start(bf16[96,1152]{1,0:T(8,128)(2,1)S(1)} %select_select_fusion.1), channel_id=1, source_target_pairs={{0,16},{4,20},{8,0},{12,4},{16,24},{20,28},{24,8},{28,12},{1,17},{... | collective-permute-start | bytes 663560 | tf_op jit(solution)/shard_map/ppermute | solution.py:19
  18.6 3.5 %collective-permute-done.7 = bf16[112,1152]{1,0:T(8,128)(2,1)S(1)} collective-permute-done((bf16[112,1152]{1,0:T(8,128)(2,1)S(1)}, bf16[112,1152]{1,0:T(8,128)(2,1)S(1)}, u32[]{:S(2)}, u32[]{:S(2)}) %collective-permute-start.7) | collective-permute-done | bytes 258080 | tf_op jit(solution)/shard_map/ppermute | solution.py:19
  22.2 0.1 collective-permute-start.8
  22.3 0.1 pad_add_fusion
  22.4 1.2 %collective-permute-done.3 = bf16[96,1152]{1,0:T(8,128)(2,1)S(1)} collective-permute-done((bf16[96,1152]{1,0:T(8,128)(2,1)S(1)}, bf16[96,1152]{1,0:T(8,128)(2,1)S(1)}, u32[]{:S(2)}, u32[]{:S(2)}) %collective-permute-start.3) | collective-permute-done | bytes 221216 | tf_op jit(solution)/shard_map/ppermute | solution.py:19
  23.6 3.4 %collective-permute-start.4 = (bf16[96,1152]{1,0:T(8,128)(2,1)S(1)}, bf16[96,1152]{1,0:T(8,128)(2,1)S(1)}, u32[]{:S(2)}, u32[]{:S(2)}) collective-permute-start(bf16[96,1152]{1,0:T(8,128)(2,1)S(1)} %collective-permute-done.3), channel_id=1, source_target_pairs={{0,16},{4,20},{8,0},{12,4},{16,24},{20,28},{24,8},{28,12},{1,17},{... | collective-permute-start | bytes 663560 | tf_op jit(solution)/shard_map/ppermute | solution.py:19
  27.0 0.1 select_select_fusion
  27.1 0.6 collective-permute-start.12
  27.7 0.7 collective-permute-start.9
  28.4 4.5 %collective-permute-done.4 = bf16[96,1152]{1,0:T(8,128)(2,1)S(1)} collective-permute-done((bf16[96,1152]{1,0:T(8,128)(2,1)S(1)}, bf16[96,1152]{1,0:T(8,128)(2,1)S(1)}, u32[]{:S(2)}, u32[]{:S(2)}) %collective-permute-start.4) | collective-permute-done | bytes 221216 | tf_op jit(solution)/shard_map/ppermute | solution.py:19
  32.9 3.4 %collective-permute-start.5 = (bf16[96,1152]{1,0:T(8,128)(2,1)S(1)}, bf16[96,1152]{1,0:T(8,128)(2,1)S(1)}, u32[]{:S(2)}, u32[]{:S(2)}) collective-permute-start(bf16[96,1152]{1,0:T(8,128)(2,1)S(1)} %collective-permute-done.4), channel_id=1, source_target_pairs={{0,16},{4,20},{8,0},{12,4},{16,24},{20,28},{24,8},{28,12},{1,17},{... | collective-permute-start | bytes 663560 | tf_op jit(solution)/shard_map/ppermute | solution.py:19
  36.3 2.1 %collective-permute-done.9 = bf16[112,1152]{1,0:T(8,128)(2,1)S(1)} collective-permute-done((bf16[112,1152]{1,0:T(8,128)(2,1)S(1)}, bf16[112,1152]{1,0:T(8,128)(2,1)S(1)}, u32[]{:S(2)}, u32[]{:S(2)}) %collective-permute-start.9) | collective-permute-done | bytes 258080 | tf_op jit(solution)/shard_map/ppermute | solution.py:19
  38.4 0.5 collective-permute-start.13
  38.9 3.4 %collective-permute-start.10 = (bf16[112,1152]{1,0:T(8,128)(2,1)S(1)}, bf16[112,1152]{1,0:T(8,128)(2,1)S(1)}, u32[]{:S(2)}, u32[]{:S(2)}) collective-permute-start(bf16[112,1152]{1,0:T(8,128)(2,1)S(1)} %collective-permute-done.9), channel_id=1, source_target_pairs={{0,16},{4,20},{8,0},{12,4},{16,24},{20,28},{24,8},{28,12},{1,17},{... | collective-permute-start | bytes 774152 | tf_op jit(solution)/shard_map/ppermute | solution.py:19
  42.3 0.8 collective-permute-done.5
  43.2 1.3 %fusion.20 = (f32[]{:T(128)}, bf16[192,384]{1,0:T(8,128)(2,1)S(1)}) fusion(s32[384]{0:T(512)S(1)} %add.198, s32[192]{0:T(256)S(1)} %pad_add_fusion, f32[]{:T(128)} %bitcast.50, bf16[384,1152]{1,0:T(8,128)(2,1)S(1)} %pad_maximum_fusion, bf16[96,1152]{1,0:T(8,128)(2,1)S(1)} %slice-done, bf16[96,1152]{1,0:T(8,128)(2,1)S(1)} %bitcast.55, f32[]{:T(128)} %bitcast), kind=kOutput, calls=%fused_computation.29 | convolution fusion | flops 172081152 | bytes 1476876 | tf_op jit(solution)/shard_map/dot_general | solution.py:12
  44.5 0.6 broadcast_in_dim.24
  45.3 0.3 convolution_multiply_fusion
  45.6 0.8 collective-permute-start.6
  46.5 0.5 collective-permute-done.10
  47.0 0.8 collective-permute-start.17
  47.8 0.8 %collective-permute-start.14 = (bf16[112,1152]{1,0:T(8,128)(2,1)S(1)}, bf16[112,1152]{1,0:T(8,128)(2,1)S(1)}, u32[]{:S(2)}, u32[]{:S(2)}) collective-permute-start(bf16[112,1152]{1,0:T(8,128)(2,1)S(1)} %collective-permute-done.10), channel_id=1, source_target_pairs={{0,4},{4,0},{8,12},{12,8},{16,20},{20,16},{24,28},{28,24},{1,5},{5... | collective-permute-start | bytes 774152 | tf_op jit(solution)/shard_map/ppermute | solution.py:19
  48.6 3.4 %collective-permute-start.11 = (bf16[112,1152]{1,0:T(8,128)(2,1)S(1)}, bf16[112,1152]{1,0:T(8,128)(2,1)S(1)}, u32[]{:S(2)}, u32[]{:S(2)}) collective-permute-start(bf16[112,1152]{1,0:T(8,128)(2,1)S(1)} %collective-permute-done.10), channel_id=1, source_target_pairs={{0,16},{4,20},{8,0},{12,4},{16,24},{20,28},{24,8},{28,12},{1,17},{... | collective-permute-start | bytes 774152 | tf_op jit(solution)/shard_map/ppermute | solution.py:19
  52.0 11.7 %collective-permute-done.14 = bf16[112,1152]{1,0:T(8,128)(2,1)S(1)} collective-permute-done((bf16[112,1152]{1,0:T(8,128)(2,1)S(1)}, bf16[112,1152]{1,0:T(8,128)(2,1)S(1)}, u32[]{:S(2)}, u32[]{:S(2)}) %collective-permute-start.14) | collective-permute-done | bytes 258080 | tf_op jit(solution)/shard_map/ppermute | solution.py:19
  63.8 0.7 collective-permute-start.18
  64.5 1.3 %collective-permute-start.15 = (bf16[112,1152]{1,0:T(8,128)(2,1)S(1)}, bf16[112,1152]{1,0:T(8,128)(2,1)S(1)}, u32[]{:S(2)}, u32[]{:S(2)}) collective-permute-start(bf16[112,1152]{1,0:T(8,128)(2,1)S(1)} %collective-permute-done.11), channel_id=1, source_target_pairs={{0,4},{4,0},{8,12},{12,8},{16,20},{20,16},{24,28},{28,24},{1,5},{5... | collective-permute-start | bytes 774152 | tf_op jit(solution)/shard_map/ppermute | solution.py:19
  65.9 1.4 %collective-permute-done.18 = f32[8,128]{1,0:T(8,128)S(1)} collective-permute-done((f32[8,128]{1,0:T(8,128)S(1)}, f32[8,128]{1,0:T(8,128)S(1)}, u32[]{:S(2)}, u32[]{:S(2)}) %collective-permute-start.18) | collective-permute-done | bytes 4128 | tf_op jit(solution)/shard_map/ppermute | solution.py:19
  67.4 2.4 %collective-permute-start.19 = (f32[8,128]{1,0:T(8,128)S(1)}, f32[8,128]{1,0:T(8,128)S(1)}, u32[]{:S(2)}, u32[]{:S(2)}) collective-permute-start(f32[8,128]{1,0:T(8,128)S(1)} %add.224), channel_id=1, source_target_pairs={{0,8},{4,12},{8,0},{12,4},{16,24},{20,28},{24,16},{28,20},{1,9},{5... | collective-permute-start | bytes 12296 | tf_op jit(solution)/shard_map/ppermute | solution.py:19
  69.8 1.6 %collective-permute-done.19 = f32[8,128]{1,0:T(8,128)S(1)} collective-permute-done((f32[8,128]{1,0:T(8,128)S(1)}, f32[8,128]{1,0:T(8,128)S(1)}, u32[]{:S(2)}, u32[]{:S(2)}) %collective-permute-start.19) | collective-permute-done | bytes 4128 | tf_op jit(solution)/shard_map/ppermute | solution.py:19
  71.4 3.0 %collective-permute-start.20 = (f32[8,128]{1,0:T(8,128)S(1)}, f32[8,128]{1,0:T(8,128)S(1)}, u32[]{:S(2)}, u32[]{:S(2)}) collective-permute-start(f32[8,128]{1,0:T(8,128)S(1)} %add.225), channel_id=1, source_target_pairs={{0,16},{4,20},{8,24},{12,28},{16,0},{20,4},{24,8},{28,12},{1,17},{... | collective-permute-start | bytes 12296 | tf_op jit(solution)/shard_map/ppermute | solution.py:19
  74.4 1.6 %collective-permute-done.20 = f32[8,128]{1,0:T(8,128)S(1)} collective-permute-done((f32[8,128]{1,0:T(8,128)S(1)}, f32[8,128]{1,0:T(8,128)S(1)}, u32[]{:S(2)}, u32[]{:S(2)}) %collective-permute-start.20) | collective-permute-done | bytes 4128 | tf_op jit(solution)/shard_map/ppermute | solution.py:19
  76.0 0.5 slice.155
  77.2 1.1 %fusion.2 = f32[1,96,1152]{2,1,0:T(8,128)} fusion(f32[96,1152]{1,0:T(8,128)S(1)} %collective-permute-done.6, bf16[384,1152]{1,0:T(8,128)(2,1)S(1)} %pad_maximum_fusion, f32[]{:T(128)} %bitcast, bf16[192,384]{1,0:T(8,128)(2,1)S(1)} %get-tuple-element.22), kind=kOutput, calls=%fused_computation.5 | convolution fusion | flops 85155840 | bytes 1843204 | tf_op jit(solution)/shard_map/dot_general | solution.py:94
  78.3 0.1 concatenate.27
  78.4 2.1 %fusion.1 = f32[1,96,1152]{2,1,0:T(8,128)} fusion(bf16[768,1152]{1,0:T(8,128)(2,1)S(1)} %slice_dynamic-update-slice_fusion, f32[]{:T(128)} %bitcast, s32[96]{0:T(128)S(1)} %iota_add_fusion.1, f32[]{:T(128)} %bitcast.51, s32[768]{0:T(1024)S(1)} %concatenate.27, bf16[1,96,1152]{2,1,0:T(8,128)(2,1)S(1)} %copy-done.1), kind=kOutput, calls=%fused_computation.4 | convolution fusion | flops 340512768 | bytes 2436488 | tf_op jit(solution)/shard_map/dot_general | solution.py:94
  (56 shorter events, 0.6 us)
Async XLA Ops:
  0.6 21.5 %copy-start = (bf16[1,96,1152]{2,1,0:T(8,128)(2,1)S(1)}, bf16[1,96,1152]{2,1,0:T(8,128)(2,1)}, u32[]{:S(2)}) copy-start(bf16[1,96,1152]{2,1,0:T(8,128)(2,1)} %param.6) | copy-start | bytes 663556
  0.6 11.8 %collective-permute-start.1 = (bf16[96,1152]{1,0:T(8,128)(2,1)}, bf16[96,1152]{1,0:T(8,128)(2,1)S(1)}, u32[]{:S(2)}, u32[]{:S(2)}) collective-permute-start(bf16[96,1152]{1,0:T(8,128)(2,1)} %bitcast.56), channel_id=1, source_target_pairs={{0,2},{1,3},{2,0},{3,1},{4,6},{5,7},{6,4},{7,5},{8,10},{9,11},{10,... | collective-permute-start | bytes 663560 | tf_op jit(solution)/shard_map/ppermute | solution.py:19
  4.3 18.0 %copy-start.3 = (s32[1,96]{1,0:T(1,128)S(1)}, s32[1,96]{1,0:T(1,128)}, u32[]{:S(2)}) copy-start(s32[1,96]{1,0:T(1,128)} %param.8) | copy-start | bytes 1156
  5.3 8.8 %collective-permute-start = (bf16[112,1152]{1,0:T(8,128)(2,1)S(1)}, bf16[112,1152]{1,0:T(8,128)(2,1)S(1)}, u32[]{:S(2)}, u32[]{:S(2)}) collective-permute-start(bf16[112,1152]{1,0:T(8,128)(2,1)S(1)} %pad_maximum_fusion.1), channel_id=1, source_target_pairs={{0,4},{4,0},{8,12},{12,8},{16,20},{20,16},{24,28},{28,24},{1,5},{5... | collective-permute-start | bytes 774152 | tf_op jit(solution)/shard_map/ppermute | solution.py:19
  13.5 1.5 %collective-permute-start.2 = (bf16[96,1152]{1,0:T(8,128)(2,1)S(1)}, bf16[96,1152]{1,0:T(8,128)(2,1)S(1)}, u32[]{:S(2)}, u32[]{:S(2)}) collective-permute-start(bf16[96,1152]{1,0:T(8,128)(2,1)S(1)} %broadcast_select_fusion.1), channel_id=1, source_target_pairs={{0,1},{1,0},{2,3},{3,2},{4,5},{5,4},{6,7},{7,6},{8,9},{9,8},{10,11... | collective-permute-start | bytes 663560 | tf_op jit(solution)/shard_map/ppermute | solution.py:19
  13.5 8.6 %collective-permute-start.7 = (bf16[112,1152]{1,0:T(8,128)(2,1)S(1)}, bf16[112,1152]{1,0:T(8,128)(2,1)S(1)}, u32[]{:S(2)}, u32[]{:S(2)}) collective-permute-start(bf16[112,1152]{1,0:T(8,128)(2,1)S(1)} %pad_maximum_fusion.1), channel_id=1, source_target_pairs={{0,2},{1,3},{2,0},{3,1},{4,6},{5,7},{6,4},{7,5},{8,10},{9,11},{10,... | collective-permute-start | bytes 774152 | tf_op jit(solution)/shard_map/ppermute | solution.py:19
  14.1 14.2 %copy-start.2 = (bf16[112,1152]{1,0:T(8,128)(2,1)}, bf16[112,1152]{1,0:T(8,128)(2,1)S(1)}, u32[]{:S(2)}) copy-start(bf16[112,1152]{1,0:T(8,128)(2,1)S(1)} %collective-permute-done) | copy-start | bytes 774148
  16.0 7.6 %collective-permute-start.3 = (bf16[96,1152]{1,0:T(8,128)(2,1)S(1)}, bf16[96,1152]{1,0:T(8,128)(2,1)S(1)}, u32[]{:S(2)}, u32[]{:S(2)}) collective-permute-start(bf16[96,1152]{1,0:T(8,128)(2,1)S(1)} %select_select_fusion.1), channel_id=1, source_target_pairs={{0,16},{4,20},{8,0},{12,4},{16,24},{20,28},{24,8},{28,12},{1,17},{... | collective-permute-start | bytes 663560 | tf_op jit(solution)/shard_map/ppermute | solution.py:19
  22.2 4.8 %collective-permute-start.8 = (bf16[112,1152]{1,0:T(8,128)(2,1)S(1)}, bf16[112,1152]{1,0:T(8,128)(2,1)S(1)}, u32[]{:S(2)}, u32[]{:S(2)}) collective-permute-start(bf16[112,1152]{1,0:T(8,128)(2,1)S(1)} %broadcast_select_fusion), channel_id=1, source_target_pairs={{0,1},{1,0},{2,3},{3,2},{4,5},{5,4},{6,7},{7,6},{8,9},{9,8},{10,11... | collective-permute-start | bytes 774152 | tf_op jit(solution)/shard_map/ppermute | solution.py:19
  23.6 9.3 %collective-permute-start.4 = (bf16[96,1152]{1,0:T(8,128)(2,1)S(1)}, bf16[96,1152]{1,0:T(8,128)(2,1)S(1)}, u32[]{:S(2)}, u32[]{:S(2)}) collective-permute-start(bf16[96,1152]{1,0:T(8,128)(2,1)S(1)} %collective-permute-done.3), channel_id=1, source_target_pairs={{0,16},{4,20},{8,0},{12,4},{16,24},{20,28},{24,8},{28,12},{1,17},{... | collective-permute-start | bytes 663560 | tf_op jit(solution)/shard_map/ppermute | solution.py:19
  27.1 9.2 %collective-permute-start.12 = (bf16[112,1152]{1,0:T(8,128)(2,1)S(1)}, bf16[112,1152]{1,0:T(8,128)(2,1)S(1)}, u32[]{:S(2)}, u32[]{:S(2)}) collective-permute-start(bf16[112,1152]{1,0:T(8,128)(2,1)S(1)} %select_select_fusion), channel_id=1, source_target_pairs={{0,4},{4,0},{8,12},{12,8},{16,20},{20,16},{24,28},{28,24},{1,5},{5... | collective-permute-start | bytes 774152 | tf_op jit(solution)/shard_map/ppermute | solution.py:19
  27.7 10.7 %collective-permute-start.9 = (bf16[112,1152]{1,0:T(8,128)(2,1)S(1)}, bf16[112,1152]{1,0:T(8,128)(2,1)S(1)}, u32[]{:S(2)}, u32[]{:S(2)}) collective-permute-start(bf16[112,1152]{1,0:T(8,128)(2,1)S(1)} %select_select_fusion), channel_id=1, source_target_pairs={{0,16},{4,20},{8,0},{12,4},{16,24},{20,28},{24,8},{28,12},{1,17},{... | collective-permute-start | bytes 774152 | tf_op jit(solution)/shard_map/ppermute | solution.py:19
  28.4 14.8 %slice-start = ((bf16[112,1152]{1,0:T(8,128)(2,1)}), bf16[96,1152]{1,0:T(8,128)(2,1)S(1)}, s32[]{:S(2)}) async-start(bf16[112,1152]{1,0:T(8,128)(2,1)} %copy-done.2), calls=%async_computation | async-start | bytes 442368 | tf_op jit(solution)/shard_map/slice | solution.py:116
  32.9 10.3 %collective-permute-start.5 = (bf16[96,1152]{1,0:T(8,128)(2,1)S(1)}, bf16[96,1152]{1,0:T(8,128)(2,1)S(1)}, u32[]{:S(2)}, u32[]{:S(2)}) collective-permute-start(bf16[96,1152]{1,0:T(8,128)(2,1)S(1)} %collective-permute-done.4), channel_id=1, source_target_pairs={{0,16},{4,20},{8,0},{12,4},{16,24},{20,28},{24,8},{28,12},{1,17},{... | collective-permute-start | bytes 663560 | tf_op jit(solution)/shard_map/ppermute | solution.py:19
  38.4 8.0 %collective-permute-start.13 = (bf16[112,1152]{1,0:T(8,128)(2,1)S(1)}, bf16[112,1152]{1,0:T(8,128)(2,1)S(1)}, u32[]{:S(2)}, u32[]{:S(2)}) collective-permute-start(bf16[112,1152]{1,0:T(8,128)(2,1)S(1)} %collective-permute-done.9), channel_id=1, source_target_pairs={{0,4},{4,0},{8,12},{12,8},{16,20},{20,16},{24,28},{28,24},{1,5},{5... | collective-permute-start | bytes 774152 | tf_op jit(solution)/shard_map/ppermute | solution.py:19
  38.9 8.0 %collective-permute-start.10 = (bf16[112,1152]{1,0:T(8,128)(2,1)S(1)}, bf16[112,1152]{1,0:T(8,128)(2,1)S(1)}, u32[]{:S(2)}, u32[]{:S(2)}) collective-permute-start(bf16[112,1152]{1,0:T(8,128)(2,1)S(1)} %collective-permute-done.9), channel_id=1, source_target_pairs={{0,16},{4,20},{8,0},{12,4},{16,24},{20,28},{24,8},{28,12},{1,17},{... | collective-permute-start | bytes 774152 | tf_op jit(solution)/shard_map/ppermute | solution.py:19
  45.2 1.2 %collective-permute-start.16 = (f32[8,128]{1,0:T(8,128)S(1)}, f32[8,128]{1,0:T(8,128)S(1)}, u32[]{:S(2)}, u32[]{:S(2)}) collective-permute-start(f32[8,128]{1,0:T(8,128)S(1)} %broadcast_in_dim.24), channel_id=1, source_target_pairs={{0,1},{1,0},{2,3},{3,2},{4,5},{5,4},{6,7},{7,6},{8,9},{9,8},{10,11... | collective-permute-start | bytes 12296 | tf_op jit(solution)/shard_map/ppermute | solution.py:19
  45.6 31.6 %collective-permute-start.6 = (f32[96,1152]{1,0:T(8,128)S(1)}, f32[96,1152]{1,0:T(8,128)S(1)}, u32[]{:S(2)}, u32[]{:S(2)}) collective-permute-start(f32[96,1152]{1,0:T(8,128)S(1)} %convolution_multiply_fusion), channel_id=1, source_target_pairs={{0,4},{4,0},{8,12},{12,8},{16,20},{20,16},{24,28},{28,24},{1,5},{5... | collective-permute-start | bytes 1327112 | tf_op jit(solution)/shard_map/ppermute | solution.py:19
  47.0 5.0 %collective-permute-start.17 = (f32[8,128]{1,0:T(8,128)S(1)}, f32[8,128]{1,0:T(8,128)S(1)}, u32[]{:S(2)}, u32[]{:S(2)}) collective-permute-start(f32[8,128]{1,0:T(8,128)S(1)} %add.222), channel_id=1, source_target_pairs={{0,2},{1,3},{2,0},{3,1},{4,6},{5,7},{6,4},{7,5},{8,10},{9,11},{10,... | collective-permute-start | bytes 12296 | tf_op jit(solution)/shard_map/ppermute | solution.py:19
  47.8 16.0 %collective-permute-start.14 = (bf16[112,1152]{1,0:T(8,128)(2,1)S(1)}, bf16[112,1152]{1,0:T(8,128)(2,1)S(1)}, u32[]{:S(2)}, u32[]{:S(2)}) collective-permute-start(bf16[112,1152]{1,0:T(8,128)(2,1)S(1)} %collective-permute-done.10), channel_id=1, source_target_pairs={{0,4},{4,0},{8,12},{12,8},{16,20},{20,16},{24,28},{28,24},{1,5},{5... | collective-permute-start | bytes 774152 | tf_op jit(solution)/shard_map/ppermute | solution.py:19
  48.6 15.9 %collective-permute-start.11 = (bf16[112,1152]{1,0:T(8,128)(2,1)S(1)}, bf16[112,1152]{1,0:T(8,128)(2,1)S(1)}, u32[]{:S(2)}, u32[]{:S(2)}) collective-permute-start(bf16[112,1152]{1,0:T(8,128)(2,1)S(1)} %collective-permute-done.10), channel_id=1, source_target_pairs={{0,16},{4,20},{8,0},{12,4},{16,24},{20,28},{24,8},{28,12},{1,17},{... | collective-permute-start | bytes 774152 | tf_op jit(solution)/shard_map/ppermute | solution.py:19
  63.8 3.6 %collective-permute-start.18 = (f32[8,128]{1,0:T(8,128)S(1)}, f32[8,128]{1,0:T(8,128)S(1)}, u32[]{:S(2)}, u32[]{:S(2)}) collective-permute-start(f32[8,128]{1,0:T(8,128)S(1)} %add.223), channel_id=1, source_target_pairs={{0,4},{4,0},{8,12},{12,8},{16,20},{20,16},{24,28},{28,24},{1,5},{5... | collective-permute-start | bytes 12296 | tf_op jit(solution)/shard_map/ppermute | solution.py:19
  64.5 13.8 %collective-permute-start.15 = (bf16[112,1152]{1,0:T(8,128)(2,1)S(1)}, bf16[112,1152]{1,0:T(8,128)(2,1)S(1)}, u32[]{:S(2)}, u32[]{:S(2)}) collective-permute-start(bf16[112,1152]{1,0:T(8,128)(2,1)S(1)} %collective-permute-done.11), channel_id=1, source_target_pairs={{0,4},{4,0},{8,12},{12,8},{16,20},{20,16},{24,28},{28,24},{1,5},{5... | collective-permute-start | bytes 774152 | tf_op jit(solution)/shard_map/ppermute | solution.py:19
  65.8 12.6 %copy-start.1 = (bf16[1,96,1152]{2,1,0:T(8,128)(2,1)S(1)}, bf16[1,96,1152]{2,1,0:T(8,128)(2,1)}, u32[]{:S(2)}) copy-start(bf16[1,96,1152]{2,1,0:T(8,128)(2,1)} %param.7) | copy-start | bytes 663556
  67.4 4.0 %collective-permute-start.19 = (f32[8,128]{1,0:T(8,128)S(1)}, f32[8,128]{1,0:T(8,128)S(1)}, u32[]{:S(2)}, u32[]{:S(2)}) collective-permute-start(f32[8,128]{1,0:T(8,128)S(1)} %add.224), channel_id=1, source_target_pairs={{0,8},{4,12},{8,0},{12,4},{16,24},{20,28},{24,16},{28,20},{1,9},{5... | collective-permute-start | bytes 12296 | tf_op jit(solution)/shard_map/ppermute | solution.py:19
  71.4 4.6 %collective-permute-start.20 = (f32[8,128]{1,0:T(8,128)S(1)}, f32[8,128]{1,0:T(8,128)S(1)}, u32[]{:S(2)}, u32[]{:S(2)}) collective-permute-start(f32[8,128]{1,0:T(8,128)S(1)} %add.225), channel_id=1, source_target_pairs={{0,16},{4,20},{8,24},{12,28},{16,0},{20,4},{24,8},{28,12},{1,17},{... | collective-permute-start | bytes 12296 | tf_op jit(solution)/shard_map/ppermute | solution.py:19
where the time goes:
time: 81.9 us; the launch traced here: 81.7 us
  starting transfers between devices  33.2 us (41%)
  waiting for transfers between devices  29.9 us (37%)
  between operations  6.61 us (8%)
  other arithmetic  5.58 us (7%)
  matrix products  4.83 us (6%)
  local copies, waits for them, and re-layouts  1.55 us (2%)
    ppermute x21, starting transfers between devices, exchange(): lax.ppermute(array, axis, [(place, mate(place)) for place in range(size)])  33.2 us
    ppermute x21, waiting for transfers between devices, exchange(): lax.ppermute(array, axis, [(place, mate(place)) for place in range(size)])  29.9 us
    dot_general x3, matrix products, grads(): return temper * jnp.dot(slopes, others, preferred_element_type=jnp.float32)  3.52 us
  transfers between devices with their start and end apart: 21, of which 11 were waited for; matrix products, arithmetic and copies ran while one was open for 12% of the time, Pallas kernels for 0%

commit v1 on v0

v1 whole, which is shorter than its diff:
```python
import jax
import jax.numpy as jnp
from jax import lax
from jax.sharding import PartitionSpec as P

TAIL = 16
DIGIT = 128


def pair_slopes(rows, others, hits, temper, offset):
    logits = temper * jnp.dot(rows, others.T, preferred_element_type=jnp.float32) + offset
    hit_values = hits.astype(jnp.float32)
    slopes = (jax.nn.sigmoid(logits) - hit_values).astype(jnp.bfloat16)
    return logits, hit_values, slopes


def exchange(array, axis, size, mate):
    return lax.ppermute(array, axis, [(place, mate(place)) for place in range(size)])


def swap(array, axis, size, bit):
    return exchange(array, axis, size, lambda place: place ^ bit)


def after(array, *earlier):
    return lax.optimization_barrier((array, *earlier))[0]


def pick(own, across, wanted, here, mate_wanted, groups):
    for_mate = jnp.where((mate_wanted ^ here) >> 1 == 0, own, across)
    from_mate = swap(for_mate, "group", groups, 1)
    held = jnp.where((wanted ^ here) >> 1 == 0, own, across)
    return jnp.where((wanted ^ here) & 1 == 0, held, from_mate)


def line_gather(own, place):
    z = place // 2

    def send(block, targets):
        return lax.ppermute(block, "blk", [(2 * source + y, 2 * target + y) for source, target in targets.items() for y in range(2)])

    two_off = send(own, {0: 2, 1: 3, 2: 0, 3: 1})
    from_below = send(own, {0: 1, 1: 2, 2: 3})
    from_above = send(own, {3: 2, 2: 1, 1: 0})
    far = send(two_off, {2: 3, 1: 0})
    near = jnp.where(z == 0, from_above, from_below)
    last = jnp.where((z == 0) | (z == 3), far, from_above)
    return [own, two_off, near, last]


def line_order(place):
    z, y = place // 2, place % 2
    near = jnp.where(z == 0, 1, z - 1)
    last = jnp.where(z == 1, 2, jnp.where(z == 3, 0, 3))
    return [2 * source + y for source in (z, z ^ 2, near, last)]


def with_labels(images, labels):
    digits = jnp.stack([labels // DIGIT, labels % DIGIT]).astype(images.dtype)
    return jnp.concatenate([images, jnp.pad(digits, ((0, TAIL - 2), (0, images.shape[1] - labels.shape[0])))])


def labels_of(block, rows):
    digits = block[rows : rows + 2, :rows].astype(jnp.int32)
    return digits[0] * DIGIT + digits[1]


def hop_sum(total, hops):
    for axis, size, bit in hops:
        total = total + swap(total, axis, size, bit)
    return total


def shards(image_embeds, text_embeds, positives, partner, log_temp, bias):
    texts = text_embeds[0]
    labels = positives[0]
    rows = texts.shape[0]
    blocks = lax.axis_size("blk")
    groups = lax.axis_size("group")
    blk_place = lax.axis_index("blk")
    group_place = lax.axis_index("group")
    images = with_labels(image_embeds[0], labels)

    def partner_of(group):
        return jnp.sum(jnp.where(jnp.arange(groups) == group, partner, 0))

    def scorer_of(group):
        return jnp.sum(jnp.where(partner == group, jnp.arange(groups), 0))

    def index_of(places):
        return (jnp.stack(places)[:, None] * rows + jnp.arange(rows)[None, :]).reshape(-1)

    def matches(some_labels, index):
        return some_labels[:, None] == index[None, :]

    def grads(slopes, others):
        return temper * jnp.dot(slopes, others, preferred_element_type=jnp.float32)

    packed = after(jnp.concatenate([images, texts]))
    tailed = images.shape[0]
    own_images, own_texts = packed[:rows], packed[tailed:]
    hops = [(axis, size, 1 << step) for axis, size in (("group", groups), ("blk", blocks)) for step in range(size.bit_length() - 1)]
    scorer = scorer_of(group_place)
    texts_across = swap(texts, "group", groups, 2)
    images_across = swap(after(packed[:tailed], texts_across), "group", groups, 2)
    partner_text = pick(own_texts, texts_across, partner_of(group_place), group_place, partner_of(group_place ^ 1), groups)
    images_across = after(images_across, partner_text)
    scorer_image = pick(packed[:tailed], images_across, scorer, group_place, scorer_of(group_place ^ 1), groups)
    log_temp, bias, blk_place, labels = lax.optimization_barrier((log_temp, bias, blk_place, labels, partner_text))[:4]
    temper = jnp.exp(log_temp[0])
    offset = bias[0]

    if blocks == 8:
        mate = swap(packed, "blk", blocks, 1)
        places = line_order(blk_place)
        text_blocks = line_gather(partner_text, blk_place)
        image_blocks = line_gather(scorer_image, blk_place)

        column_texts = jnp.concatenate(text_blocks)
        two_images = jnp.concatenate([own_images, mate[:rows]])
        two_labels = jnp.concatenate([labels, labels_of(mate, rows)])
        hits = matches(two_labels, index_of(places))
        logits, hit_values, slopes = pair_slopes(two_images, column_texts, hits, temper, offset)
        total = jnp.sum(jax.nn.softplus(logits) - hit_values * logits)
        total = hop_sum(jnp.full((8, 128), total), hops[:3])
        image_part = swap(grads(slopes[rows:], column_texts), "blk", blocks, 1)
        image_grads = grads(slopes[:rows], column_texts) + image_part

        column_images = after(jnp.concatenate([block[:rows] for block in image_blocks]), total)
        column_labels = jnp.concatenate([labels_of(block, rows) for block in image_blocks])
        two_texts = jnp.concatenate([own_texts, mate[tailed:]])
        back_hits = matches(index_of([blk_place, blk_place ^ 1]), column_labels)
        back_slopes = pair_slopes(two_texts, column_images, back_hits, temper, offset)[2]
        text_part = swap(grads(back_slopes[rows:], column_images), "blk", blocks, 1)
        text_grads = grads(back_slopes[:rows], column_images) + text_part
    else:
        all_texts = lax.all_gather(partner_text, "blk", axis=0, tiled=True)
        every_image = lax.all_gather(scorer_image, "blk", axis=0)
        hits = matches(labels, jnp.arange(blocks * rows))
        logits, hit_values, slopes = pair_slopes(own_images, all_texts, hits, temper, offset)
        total = jnp.sum(jax.nn.softplus(logits) - hit_values * logits)
        total = hop_sum(jnp.full((8, 128), total), hops[:3])
        image_grads = grads(slopes, all_texts)
        all_images = every_image[:, :rows].reshape(blocks * rows, -1)
        back_labels = jax.vmap(lambda block: labels_of(block, rows))(every_image).reshape(-1)
        back_hits = matches(index_of([blk_place]), back_labels)
        back_slopes = pair_slopes(own_texts, all_images, back_hits, temper, offset)[2]
        text_grads = grads(back_slopes, all_images)

    total = hop_sum(total, hops[3:])
    loss = total[0, :1] / (groups * rows * blocks * blocks)
    return (image_grads[None], text_grads[None], loss)


def solution(mesh):
    in_specs = (P("group", "blk", None), P("group", "blk", None), P("group", "blk"), P(), P(), P())
    out_specs = (P("group", "blk", None), P("group", "blk", None), P())
    return jax.shard_map(shards, mesh=mesh, in_specs=in_specs, out_specs=out_specs, check_vma=False)
```

time: 81.9 us -> 76.1 us (0.929)
  waiting for transfers between devices: 29.9 us -> 25.5 us
  starting transfers between devices: 33.2 us -> 32.2 us
    ppermute x21 -> x12, starting transfers between devices: 33.2 us -> 11.5 us  [exchange(): lax.ppermute(array, axis, [(place, mate(place)) for place in range(size)])]
    ppermute x0 -> x8, starting transfers between devices: none -> 20.7 us  [send(): lax.ppermute(block, 'blk', [(2 * source + y, 2 * target + y) for source,...]
    ppermute x21 -> x12, waiting for transfers between devices: 29.9 us -> 13.8 us  [exchange(): lax.ppermute(array, axis, [(place, mate(place)) for place in range(size)])]
    ppermute x0 -> x8, waiting for transfers between devices: none -> 11.6 us  [send(): lax.ppermute(block, 'blk', [(2 * source + y, 2 * target + y) for source,...]
    add x5, other arithmetic: 0.02 us -> 1.31 us  [hop_sum(): total = total + swap(total, axis, size, bit)]
    select_n x2 -> x1, other arithmetic: 1.08 us -> 0.07 us  [pick(): return jnp.where((wanted ^ here) & 1 == 0, held, from_mate)]
    select_n x2, other arithmetic: 1.05 us -> 0.07 us  [pick(): for_mate = jnp.where((mate_wanted ^ here) >> 1 == 0, own, across)]
    dot_general x3 -> x4, matrix products: 3.52 us -> 2.79 us  [grads(): return temper * jnp.dot(slopes, others, preferred_element_type=jnp.float32)]
  transfers between devices with their start and end apart: 21 -> 20, of which waited for: 11 -> 8; matrix products, arithmetic and copies ran while one was open for 12% -> 14% of each run, Pallas kernels for 0% -> 0%
where the time goes in v1:
time: 76.1 us; the launch traced here: 75.7 us
  starting transfers between devices  32.2 us (42%)
  waiting for transfers between devices  25.5 us (34%)
  between operations  6.74 us (9%)
  other arithmetic  5.31 us (7%)
  matrix products  4.61 us (6%)
  local copies, waits for them, and re-layouts  1.47 us (2%)
    ppermute x8, starting transfers between devices, send(): lax.ppermute(block, 'blk', [(2 * source + y, 2 * target + y) for source,...  20.7 us
    ppermute x12, waiting for transfers between devices, exchange(): lax.ppermute(array, axis, [(place, mate(place)) for place in range(size)])  13.8 us
    ppermute x8, waiting for transfers between devices, send(): lax.ppermute(block, 'blk', [(2 * source + y, 2 * target + y) for source,...  11.6 us
    ppermute x12, starting transfers between devices, exchange(): lax.ppermute(array, axis, [(place, mate(place)) for place in range(size)])  11.5 us
    dot_general x4, matrix products, grads(): return temper * jnp.dot(slopes, others, preferred_element_type=jnp.float32)  2.79 us
    dot_general x2, matrix products, pair_slopes(): jnp.dot(rows, others.T, preferred_element_type=jnp.float32)  1.82 us
  transfers between devices with their start and end apart: 20, of which 8 were waited for; matrix products, arithmetic and copies ran while one was open for 14% of the time, Pallas kernels for 0%

profile of v1, /device:TPU:0, one launch (start us, length us, event | category | flops | bytes accessed | tf_op | source)
XLA Modules:
  0.0 75.7 jit_solution(3616826134103151482)
XLA Ops:
  0.6 3.0 %collective-permute-start = (bf16[96,1152]{1,0:T(8,128)(2,1)}, bf16[96,1152]{1,0:T(8,128)(2,1)S(1)}, u32[]{:S(2)}, u32[]{:S(2)}) collective-permute-start(bf16[96,1152]{1,0:T(8,128)(2,1)} %bitcast.32), channel_id=1, source_target_pairs={{0,2},{1,3},{2,0},{3,1},{4,6},{5,7},{6,4},{7,5},{8,10},{9,11},{10,... | collective-permute-start | bytes 663560 | tf_op jit(solution)/shard_map/ppermute | solution.py:18
  3.6 1.4 %fusion.35 = (s32[]{:T(128)}, s32[]{:T(128)}, s32[]{:T(128)}, s32[]{:T(128)}) fusion(s32[4]{0:T(128)} %param.9, s32[]{:T(128)S(6)} %axis_index.25, s32[]{:T(128)S(6)} %xor.25), kind=kLoop, calls=%fused_computation.71 | loop fusion | flops 44 | bytes 40 | tf_op jit(solution)/shard_map/reduce_sum | solution.py:88
  5.6 0.7 fusion.37
  6.3 1.1 %pad_maximum_fusion.2 = bf16[208,1152]{1,0:T(8,128)(2,1)S(1)} fusion(bf16[96,1152]{1,0:T(8,128)(2,1)} %bitcast.33, bf16[16,1152]{1,0:T(8,128)(2,1)S(1)} %fusion.31, bf16[96,1152]{1,0:T(8,128)(2,1)} %bitcast.31), kind=kLoop, calls=%fused_computation.21 | loop fusion | flops 1437696 | bytes 958464 | tf_op jit(solution)/shard_map/concatenate | solution.py:99
  7.4 1.9 %collective-permute-done = bf16[96,1152]{1,0:T(8,128)(2,1)S(1)} collective-permute-done((bf16[96,1152]{1,0:T(8,128)(2,1)}, bf16[96,1152]{1,0:T(8,128)(2,1)S(1)}, u32[]{:S(2)}, u32[]{:S(2)}) %collective-permute-start) | collective-permute-done | bytes 221216 | tf_op jit(solution)/shard_map/ppermute | solution.py:18
  9.3 0.1 collective-permute-start.1
  9.4 1.8 %collective-permute-start.2 = (bf16[208,1152]{1,0:T(8,128)(2,1)S(1)}, bf16[208,1152]{1,0:T(8,128)(2,1)S(1)}, u32[]{:S(2)}, u32[]{:S(2)}) collective-permute-start(bf16[208,1152]{1,0:T(8,128)(2,1)S(1)} %pad_maximum_fusion.2), channel_id=1, source_target_pairs={{0,4},{4,0},{8,12},{12,8},{16,20},{20,16},{24,28},{28,24},{1,5},{5... | collective-permute-start | bytes 1437704 | tf_op jit(solution)/shard_map/ppermute | solution.py:18
  14.5 1.6 %collective-permute-start.8 = (bf16[112,1152]{1,0:T(8,128)(2,1)S(1)}, bf16[112,1152]{1,0:T(8,128)(2,1)S(1)}, u32[]{:S(2)}, u32[]{:S(2)}) collective-permute-start(bf16[112,1152]{1,0:T(8,128)(2,1)S(1)} %slice.124), channel_id=1, source_target_pairs={{0,2},{1,3},{2,0},{3,1},{4,6},{5,7},{6,4},{7,5},{8,10},{9,11},{10,... | collective-permute-start | bytes 774152 | tf_op jit(solution)/shard_map/ppermute | solution.py:18
  16.2 2.7 %collective-permute-start.3 = (bf16[96,1152]{1,0:T(8,128)(2,1)S(1)}, bf16[96,1152]{1,0:T(8,128)(2,1)S(1)}, u32[]{:S(2)}, u32[]{:S(2)}) collective-permute-start(bf16[96,1152]{1,0:T(8,128)(2,1)S(1)} %get-tuple-element.22), channel_id=1, source_target_pairs={{0,16},{4,20},{8,24},{12,28},{16,0},{20,4},{24,8},{28,12},{1,17},{... | collective-permute-start | bytes 663560 | tf_op jit(solution)/shard_map/ppermute | solution.py:40
  18.8 1.3 %collective-permute-start.4 = (bf16[96,1152]{1,0:T(8,128)(2,1)S(1)}, bf16[96,1152]{1,0:T(8,128)(2,1)S(1)}, u32[]{:S(2)}, u32[]{:S(2)}) collective-permute-start(bf16[96,1152]{1,0:T(8,128)(2,1)S(1)} %get-tuple-element.22), channel_id=1, source_target_pairs={{24,16},{28,20},{16,8},{20,12},{8,0},{12,4},{25,17},{29,21},{17,9}... | collective-permute-start | bytes 663560 | tf_op jit(solution)/shard_map/ppermute | solution.py:40
  20.1 4.6 %collective-permute-start.5 = (bf16[96,1152]{1,0:T(8,128)(2,1)S(1)}, bf16[96,1152]{1,0:T(8,128)(2,1)S(1)}, u32[]{:S(2)}, u32[]{:S(2)}) collective-permute-start(bf16[96,1152]{1,0:T(8,128)(2,1)S(1)} %get-tuple-element.22), channel_id=1, source_target_pairs={{0,8},{4,12},{8,16},{12,20},{16,24},{20,28},{1,9},{5,13},{9,17},{1... | collective-permute-start | bytes 663560 | tf_op jit(solution)/shard_map/ppermute | solution.py:40
  24.7 0.1 add_multiply_fusion
  24.8 0.1 iota_add_fusion
  24.9 0.1 add_multiply_fusion.1
  24.9 0.1 add.154
  25.0 0.1 iota_add_fusion.1
  25.1 0.1 add.165
  25.2 0.1 collective-permute-start.9
  25.4 0.1 pad_add_fusion.1
  25.5 4.7 %collective-permute-done.3 = bf16[96,1152]{1,0:T(8,128)(2,1)S(1)} collective-permute-done((bf16[96,1152]{1,0:T(8,128)(2,1)S(1)}, bf16[96,1152]{1,0:T(8,128)(2,1)S(1)}, u32[]{:S(2)}, u32[]{:S(2)}) %collective-permute-start.3) | collective-permute-done | bytes 221216 | tf_op jit(solution)/shard_map/ppermute | solution.py:40
  30.2 1.3 %collective-permute-start.6 = (bf16[96,1152]{1,0:T(8,128)(2,1)S(1)}, bf16[96,1152]{1,0:T(8,128)(2,1)S(1)}, u32[]{:S(2)}, u32[]{:S(2)}) collective-permute-start(bf16[96,1152]{1,0:T(8,128)(2,1)S(1)} %collective-permute-done.3), channel_id=1, source_target_pairs={{16,24},{20,28},{8,0},{12,4},{17,25},{21,29},{9,1},{13,5},{18,26},... | collective-permute-start | bytes 663560 | tf_op jit(solution)/shard_map/ppermute | solution.py:40
  31.6 3.8 %collective-permute-start.10 = (bf16[112,1152]{1,0:T(8,128)(2,1)S(1)}, bf16[112,1152]{1,0:T(8,128)(2,1)S(1)}, u32[]{:S(2)}, u32[]{:S(2)}) collective-permute-start(bf16[112,1152]{1,0:T(8,128)(2,1)S(1)} %select_select_fusion), channel_id=1, source_target_pairs={{0,16},{4,20},{8,24},{12,28},{16,0},{20,4},{24,8},{28,12},{1,17},{... | collective-permute-start | bytes 774152 | tf_op jit(solution)/shard_map/ppermute | solution.py:40
  35.4 1.3 %collective-permute-start.11 = (bf16[112,1152]{1,0:T(8,128)(2,1)S(1)}, bf16[112,1152]{1,0:T(8,128)(2,1)S(1)}, u32[]{:S(2)}, u32[]{:S(2)}) collective-permute-start(bf16[112,1152]{1,0:T(8,128)(2,1)S(1)} %select_select_fusion), channel_id=1, source_target_pairs={{24,16},{28,20},{16,8},{20,12},{8,0},{12,4},{25,17},{29,21},{17,9}... | collective-permute-start | bytes 774152 | tf_op jit(solution)/shard_map/ppermute | solution.py:40
  36.6 4.6 %collective-permute-start.12 = (bf16[112,1152]{1,0:T(8,128)(2,1)S(1)}, bf16[112,1152]{1,0:T(8,128)(2,1)S(1)}, u32[]{:S(2)}, u32[]{:S(2)}) collective-permute-start(bf16[112,1152]{1,0:T(8,128)(2,1)S(1)} %select_select_fusion), channel_id=1, source_target_pairs={{0,8},{4,12},{8,16},{12,20},{16,24},{20,28},{1,9},{5,13},{9,17},{1... | collective-permute-start | bytes 774152 | tf_op jit(solution)/shard_map/ppermute | solution.py:40
  41.3 1.3 %fusion.21 = (f32[]{:T(128)}, bf16[192,384]{1,0:T(8,128)(2,1)S(1)}) fusion(s32[384]{0:T(512)S(1)} %add.154, s32[192]{0:T(256)S(1)} %pad_add_fusion.1, f32[]{:T(128)} %bitcast.29, bf16[96,1152]{1,0:T(8,128)(2,1)S(1)} %get-tuple-element.31, bf16[96,1152]{1,0:T(8,128)(2,1)S(1)} %get-tuple-element.30, bf16[96,1152]{1,0:T(8,128)(2,1)S(1)} %collective-permute-done.3, ...), kind=kOutput, calls=%fused_computation.33 | convolution fusion | flops 175620096 | bytes 1476876 | tf_op jit(solution)/shard_map/dot_general | solution.py:11
  42.6 0.6 broadcast_in_dim.24
  43.3 0.1 collective-permute-start.14
  43.4 1.1 %collective-permute-done.14 = f32[8,128]{1,0:T(8,128)S(1)} collective-permute-done((f32[8,128]{1,0:T(8,128)S(1)}, f32[8,128]{1,0:T(8,128)S(1)}, u32[]{:S(2)}, u32[]{:S(2)}) %collective-permute-start.14) | collective-permute-done | bytes 4128 | tf_op jit(solution)/shard_map/ppermute | solution.py:18
  44.5 0.6 broadcast_add_fusion
  45.2 0.6 collective-permute-start.15
  45.8 3.0 %collective-permute-done.15 = f32[8,128]{1,0:T(8,128)S(1)} collective-permute-done((f32[8,128]{1,0:T(8,128)S(1)}, f32[8,128]{1,0:T(8,128)S(1)}, u32[]{:S(2)}, u32[]{:S(2)}) %collective-permute-start.15) | collective-permute-done | bytes 4128 | tf_op jit(solution)/shard_map/ppermute | solution.py:18
  48.8 0.6 fusion.45
  49.5 0.6 collective-permute-start.16
  50.1 0.3 convolution_multiply_fusion.2
  50.4 1.6 %collective-permute-start.7 = (f32[96,1152]{1,0:T(8,128)S(1)}, f32[96,1152]{1,0:T(8,128)S(1)}, u32[]{:S(2)}, u32[]{:S(2)}) collective-permute-start(f32[96,1152]{1,0:T(8,128)S(1)} %convolution_multiply_fusion.2), channel_id=1, source_target_pairs={{0,4},{4,0},{8,12},{12,8},{16,20},{20,16},{24,28},{28,24},{1,5},{5... | collective-permute-start | bytes 1327112 | tf_op jit(solution)/shard_map/ppermute | solution.py:18
  52.0 1.2 %collective-permute-done.16 = f32[8,128]{1,0:T(8,128)S(1)} collective-permute-done((f32[8,128]{1,0:T(8,128)S(1)}, f32[8,128]{1,0:T(8,128)S(1)}, u32[]{:S(2)}, u32[]{:S(2)}) %collective-permute-start.16) | collective-permute-done | bytes 4128 | tf_op jit(solution)/shard_map/ppermute | solution.py:18
  53.2 1.3 %collective-permute-start.13 = (bf16[112,1152]{1,0:T(8,128)(2,1)S(1)}, bf16[112,1152]{1,0:T(8,128)(2,1)S(1)}, u32[]{:S(2)}, u32[]{:S(2)}) collective-permute-start(bf16[112,1152]{1,0:T(8,128)(2,1)S(1)} %collective-permute-done.10), channel_id=1, source_target_pairs={{16,24},{20,28},{8,0},{12,4},{17,25},{21,29},{9,1},{13,5},{18,26},... | collective-permute-start | bytes 774152 | tf_op jit(solution)/shard_map/ppermute | solution.py:40
  54.6 6.8 %collective-permute-done.13 = bf16[112,1152]{1,0:T(8,128)(2,1)S(1)} collective-permute-done((bf16[112,1152]{1,0:T(8,128)(2,1)S(1)}, bf16[112,1152]{1,0:T(8,128)(2,1)S(1)}, u32[]{:S(2)}, u32[]{:S(2)}) %collective-permute-start.13) | collective-permute-done | bytes 258080 | tf_op jit(solution)/shard_map/ppermute | solution.py:40
  61.7 0.1 pad_add_fusion
  61.8 0.5 fusion.11
  62.3 0.3 convolution_multiply_fusion
  62.6 0.6 collective-permute-start.17
  63.2 3.6 %collective-permute-done.18 = f32[8,128]{1,0:T(8,128)S(1)} collective-permute-done((f32[8,128]{1,0:T(8,128)S(1)}, f32[8,128]{1,0:T(8,128)S(1)}, u32[]{:S(2)}, u32[]{:S(2)}) %collective-permute-start.18) | collective-permute-done | bytes 4128 | tf_op jit(solution)/shard_map/ppermute | solution.py:18
  66.8 1.6 %collective-permute-start.19 = (f32[8,128]{1,0:T(8,128)S(1)}, f32[8,128]{1,0:T(8,128)S(1)}, u32[]{:S(2)}, u32[]{:S(2)}) collective-permute-start(f32[8,128]{1,0:T(8,128)S(1)} %add.175), channel_id=1, source_target_pairs={{0,16},{4,20},{8,24},{12,28},{16,0},{20,4},{24,8},{28,12},{1,17},{... | collective-permute-start | bytes 12296 | tf_op jit(solution)/shard_map/ppermute | solution.py:18
  68.3 2.9 %collective-permute-done.19 = f32[8,128]{1,0:T(8,128)S(1)} collective-permute-done((f32[8,128]{1,0:T(8,128)S(1)}, f32[8,128]{1,0:T(8,128)S(1)}, u32[]{:S(2)}, u32[]{:S(2)}) %collective-permute-start.19) | collective-permute-done | bytes 4128 | tf_op jit(solution)/shard_map/ppermute | solution.py:18
  71.3 0.5 slice.116
  72.4 1.1 %fusion.2 = f32[1,96,1152]{2,1,0:T(8,128)} fusion(f32[96,1152]{1,0:T(8,128)S(1)} %collective-permute-done.7, f32[]{:T(128)} %bitcast.3, bf16[192,384]{1,0:T(8,128)(2,1)S(1)} %get-tuple-element.27, bf16[96,1152]{1,0:T(8,128)(2,1)S(1)} %get-tuple-element.31, bf16[96,1152]{1,0:T(8,128)(2,1)S(1)} %get-tuple-element.30, ...), kind=kOutput, calls=%fused_computation.6 | convolution fusion | flops 88694784 | bytes 1843204 | tf_op jit(solution)/shard_map/dot_general | solution.py:97
  73.5 1.1 %fusion.3 = f32[1,96,1152]{2,1,0:T(8,128)} fusion(f32[96,1152]{1,0:T(8,128)S(1)} %collective-permute-done.17, bf16[384,1152]{1,0:T(8,128)(2,1)S(1)} %pad_maximum_fusion.1, f32[]{:T(128)} %bitcast.3, bf16[192,384]{1,0:T(8,128)(2,1)S(1)} %fusion.11), kind=kOutput, calls=%fused_computation.7 | convolution fusion | flops 85155840 | bytes 1843204 | tf_op jit(solution)/shard_map/dot_general | solution.py:97
  (41 shorter events, 0.6 us)
Async XLA Ops:
  0.6 8.6 %collective-permute-start = (bf16[96,1152]{1,0:T(8,128)(2,1)}, bf16[96,1152]{1,0:T(8,128)(2,1)S(1)}, u32[]{:S(2)}, u32[]{:S(2)}) collective-permute-start(bf16[96,1152]{1,0:T(8,128)(2,1)} %bitcast.32), channel_id=1, source_target_pairs={{0,2},{1,3},{2,0},{3,1},{4,6},{5,7},{6,4},{7,5},{8,10},{9,11},{10,... | collective-permute-start | bytes 663560 | tf_op jit(solution)/shard_map/ppermute | solution.py:18
  9.3 6.8 %collective-permute-start.1 = (bf16[96,1152]{1,0:T(8,128)(2,1)S(1)}, bf16[96,1152]{1,0:T(8,128)(2,1)S(1)}, u32[]{:S(2)}, u32[]{:S(2)}) collective-permute-start(bf16[96,1152]{1,0:T(8,128)(2,1)S(1)} %broadcast_select_fusion.5), channel_id=1, source_target_pairs={{0,1},{1,0},{2,3},{3,2},{4,5},{5,4},{6,7},{7,6},{8,9},{9,8},{10,11... | collective-permute-start | bytes 663560 | tf_op jit(solution)/shard_map/ppermute | solution.py:18
  9.4 15.9 %collective-permute-start.2 = (bf16[208,1152]{1,0:T(8,128)(2,1)S(1)}, bf16[208,1152]{1,0:T(8,128)(2,1)S(1)}, u32[]{:S(2)}, u32[]{:S(2)}) collective-permute-start(bf16[208,1152]{1,0:T(8,128)(2,1)S(1)} %pad_maximum_fusion.2), channel_id=1, source_target_pairs={{0,4},{4,0},{8,12},{12,8},{16,20},{20,16},{24,28},{28,24},{1,5},{5... | collective-permute-start | bytes 1437704 | tf_op jit(solution)/shard_map/ppermute | solution.py:18
  14.5 10.7 %collective-permute-start.8 = (bf16[112,1152]{1,0:T(8,128)(2,1)S(1)}, bf16[112,1152]{1,0:T(8,128)(2,1)S(1)}, u32[]{:S(2)}, u32[]{:S(2)}) collective-permute-start(bf16[112,1152]{1,0:T(8,128)(2,1)S(1)} %slice.124), channel_id=1, source_target_pairs={{0,2},{1,3},{2,0},{3,1},{4,6},{5,7},{6,4},{7,5},{8,10},{9,11},{10,... | collective-permute-start | bytes 774152 | tf_op jit(solution)/shard_map/ppermute | solution.py:18
  16.2 9.2 %copy-start = (s32[1,96]{1,0:T(1,128)S(1)}, s32[1,96]{1,0:T(1,128)}, u32[]{:S(2)}) copy-start(s32[1,96]{1,0:T(1,128)} %param.8) | copy-start | bytes 1156
  16.2 14.0 %collective-permute-start.3 = (bf16[96,1152]{1,0:T(8,128)(2,1)S(1)}, bf16[96,1152]{1,0:T(8,128)(2,1)S(1)}, u32[]{:S(2)}, u32[]{:S(2)}) collective-permute-start(bf16[96,1152]{1,0:T(8,128)(2,1)S(1)} %get-tuple-element.22), channel_id=1, source_target_pairs={{0,16},{4,20},{8,24},{12,28},{16,0},{20,4},{24,8},{28,12},{1,17},{... | collective-permute-start | bytes 663560 | tf_op jit(solution)/shard_map/ppermute | solution.py:40
  18.8 17.8 %collective-permute-start.4 = (bf16[96,1152]{1,0:T(8,128)(2,1)S(1)}, bf16[96,1152]{1,0:T(8,128)(2,1)S(1)}, u32[]{:S(2)}, u32[]{:S(2)}) collective-permute-start(bf16[96,1152]{1,0:T(8,128)(2,1)S(1)} %get-tuple-element.22), channel_id=1, source_target_pairs={{24,16},{28,20},{16,8},{20,12},{8,0},{12,4},{25,17},{29,21},{17,9}... | collective-permute-start | bytes 663560 | tf_op jit(solution)/shard_map/ppermute | solution.py:40
  20.1 21.1 %collective-permute-start.5 = (bf16[96,1152]{1,0:T(8,128)(2,1)S(1)}, bf16[96,1152]{1,0:T(8,128)(2,1)S(1)}, u32[]{:S(2)}, u32[]{:S(2)}) collective-permute-start(bf16[96,1152]{1,0:T(8,128)(2,1)S(1)} %get-tuple-element.22), channel_id=1, source_target_pairs={{0,8},{4,12},{8,16},{12,20},{16,24},{20,28},{1,9},{5,13},{9,17},{1... | collective-permute-start | bytes 663560 | tf_op jit(solution)/shard_map/ppermute | solution.py:40
  25.2 6.3 %collective-permute-start.9 = (bf16[112,1152]{1,0:T(8,128)(2,1)S(1)}, bf16[112,1152]{1,0:T(8,128)(2,1)S(1)}, u32[]{:S(2)}, u32[]{:S(2)}) collective-permute-start(bf16[112,1152]{1,0:T(8,128)(2,1)S(1)} %broadcast_select_fusion.2), channel_id=1, source_target_pairs={{0,1},{1,0},{2,3},{3,2},{4,5},{5,4},{6,7},{7,6},{8,9},{9,8},{10,11... | collective-permute-start | bytes 774152 | tf_op jit(solution)/shard_map/ppermute | solution.py:18
  30.2 11.0 %collective-permute-start.6 = (bf16[96,1152]{1,0:T(8,128)(2,1)S(1)}, bf16[96,1152]{1,0:T(8,128)(2,1)S(1)}, u32[]{:S(2)}, u32[]{:S(2)}) collective-permute-start(bf16[96,1152]{1,0:T(8,128)(2,1)S(1)} %collective-permute-done.3), channel_id=1, source_target_pairs={{16,24},{20,28},{8,0},{12,4},{17,25},{21,29},{9,1},{13,5},{18,26},... | collective-permute-start | bytes 663560 | tf_op jit(solution)/shard_map/ppermute | solution.py:40
  31.6 21.6 %collective-permute-start.10 = (bf16[112,1152]{1,0:T(8,128)(2,1)S(1)}, bf16[112,1152]{1,0:T(8,128)(2,1)S(1)}, u32[]{:S(2)}, u32[]{:S(2)}) collective-permute-start(bf16[112,1152]{1,0:T(8,128)(2,1)S(1)} %select_select_fusion), channel_id=1, source_target_pairs={{0,16},{4,20},{8,24},{12,28},{16,0},{20,4},{24,8},{28,12},{1,17},{... | collective-permute-start | bytes 774152 | tf_op jit(solution)/shard_map/ppermute | solution.py:40
  35.4 19.2 %collective-permute-start.11 = (bf16[112,1152]{1,0:T(8,128)(2,1)S(1)}, bf16[112,1152]{1,0:T(8,128)(2,1)S(1)}, u32[]{:S(2)}, u32[]{:S(2)}) collective-permute-start(bf16[112,1152]{1,0:T(8,128)(2,1)S(1)} %select_select_fusion), channel_id=1, source_target_pairs={{24,16},{28,20},{16,8},{20,12},{8,0},{12,4},{25,17},{29,21},{17,9}... | collective-permute-start | bytes 774152 | tf_op jit(solution)/shard_map/ppermute | solution.py:40
  36.6 17.9 %collective-permute-start.12 = (bf16[112,1152]{1,0:T(8,128)(2,1)S(1)}, bf16[112,1152]{1,0:T(8,128)(2,1)S(1)}, u32[]{:S(2)}, u32[]{:S(2)}) collective-permute-start(bf16[112,1152]{1,0:T(8,128)(2,1)S(1)} %select_select_fusion), channel_id=1, source_target_pairs={{0,8},{4,12},{8,16},{12,20},{16,24},{20,28},{1,9},{5,13},{9,17},{1... | collective-permute-start | bytes 774152 | tf_op jit(solution)/shard_map/ppermute | solution.py:40
  43.3 1.2 %collective-permute-start.14 = (f32[8,128]{1,0:T(8,128)S(1)}, f32[8,128]{1,0:T(8,128)S(1)}, u32[]{:S(2)}, u32[]{:S(2)}) collective-permute-start(f32[8,128]{1,0:T(8,128)S(1)} %broadcast_in_dim.24), channel_id=1, source_target_pairs={{0,1},{1,0},{2,3},{3,2},{4,5},{5,4},{6,7},{7,6},{8,9},{9,8},{10,11... | collective-permute-start | bytes 12296 | tf_op jit(solution)/shard_map/ppermute | solution.py:18
  45.2 3.7 %collective-permute-start.15 = (f32[8,128]{1,0:T(8,128)S(1)}, f32[8,128]{1,0:T(8,128)S(1)}, u32[]{:S(2)}, u32[]{:S(2)}) collective-permute-start(f32[8,128]{1,0:T(8,128)S(1)} %broadcast_add_fusion), channel_id=1, source_target_pairs={{0,2},{1,3},{2,0},{3,1},{4,6},{5,7},{6,4},{7,5},{8,10},{9,11},{10,... | collective-permute-start | bytes 12296 | tf_op jit(solution)/shard_map/ppermute | solution.py:18
  49.5 3.7 %collective-permute-start.16 = (f32[8,128]{1,0:T(8,128)S(1)}, f32[8,128]{1,0:T(8,128)S(1)}, u32[]{:S(2)}, u32[]{:S(2)}) collective-permute-start(f32[8,128]{1,0:T(8,128)S(1)} %fusion.45), channel_id=1, source_target_pairs={{0,4},{4,0},{8,12},{12,8},{16,20},{20,16},{24,28},{28,24},{1,5},{5... | collective-permute-start | bytes 12296 | tf_op jit(solution)/shard_map/ppermute | solution.py:18
  50.4 22.1 %collective-permute-start.7 = (f32[96,1152]{1,0:T(8,128)S(1)}, f32[96,1152]{1,0:T(8,128)S(1)}, u32[]{:S(2)}, u32[]{:S(2)}) collective-permute-start(f32[96,1152]{1,0:T(8,128)S(1)} %convolution_multiply_fusion.2), channel_id=1, source_target_pairs={{0,4},{4,0},{8,12},{12,8},{16,20},{20,16},{24,28},{28,24},{1,5},{5... | collective-permute-start | bytes 1327112 | tf_op jit(solution)/shard_map/ppermute | solution.py:18
  53.2 8.2 %collective-permute-start.13 = (bf16[112,1152]{1,0:T(8,128)(2,1)S(1)}, bf16[112,1152]{1,0:T(8,128)(2,1)S(1)}, u32[]{:S(2)}, u32[]{:S(2)}) collective-permute-start(bf16[112,1152]{1,0:T(8,128)(2,1)S(1)} %collective-permute-done.10), channel_id=1, source_target_pairs={{16,24},{20,28},{8,0},{12,4},{17,25},{21,29},{9,1},{13,5},{18,26},... | collective-permute-start | bytes 774152 | tf_op jit(solution)/shard_map/ppermute | solution.py:40
  62.6 11.0 %collective-permute-start.17 = (f32[96,1152]{1,0:T(8,128)S(1)}, f32[96,1152]{1,0:T(8,128)S(1)}, u32[]{:S(2)}, u32[]{:S(2)}) collective-permute-start(f32[96,1152]{1,0:T(8,128)S(1)} %convolution_multiply_fusion), channel_id=1, source_target_pairs={{0,4},{4,0},{8,12},{12,8},{16,20},{20,16},{24,28},{28,24},{1,5},{5... | collective-permute-start | bytes 1327112 | tf_op jit(solution)/shard_map/ppermute | solution.py:18
  63.1 3.6 %collective-permute-start.18 = (f32[8,128]{1,0:T(8,128)S(1)}, f32[8,128]{1,0:T(8,128)S(1)}, u32[]{:S(2)}, u32[]{:S(2)}) collective-permute-start(f32[8,128]{1,0:T(8,128)S(1)} %add.159), channel_id=1, source_target_pairs={{0,8},{4,12},{8,0},{12,4},{16,24},{20,28},{24,16},{28,20},{1,9},{5... | collective-permute-start | bytes 12296 | tf_op jit(solution)/shard_map/ppermute | solution.py:18
  66.8 4.5 %collective-permute-start.19 = (f32[8,128]{1,0:T(8,128)S(1)}, f32[8,128]{1,0:T(8,128)S(1)}, u32[]{:S(2)}, u32[]{:S(2)}) collective-permute-start(f32[8,128]{1,0:T(8,128)S(1)} %add.175), channel_id=1, source_target_pairs={{0,16},{4,20},{8,24},{12,28},{16,0},{20,4},{24,8},{28,12},{1,17},{... | collective-permute-start | bytes 12296 | tf_op jit(solution)/shard_map/ppermute | solution.py:18
